TPU v7x, 512 devices: a whole 4x8x8 slice. The times are simulated.
512 devices in a mesh: row: 16 (over z_lo, x, core), col: 32 (over z_hi, y).
Axes of the slice: x: 4, y: 8, z: 8 (z_hi: 4, z_lo: 2; z = z_hi * 2 + z_lo), core: 2. Of those that a mesh axis runs over, the one named last changes fastest.
Arguments:
- inputs: bfloat16 [256, 12288], P('col', 'row'), may hold values from -6 to 6
- weight: bfloat16 [12288, 24576], P('row', 'col'), may hold values from -0.0546875 to 0.0546875
- hidden_bias: float32 [24576], P('col'), may hold values from -3 to 3
- cotangent: bfloat16 [256, 24576], P('row', 'col'), may hold values from -6 to 6
Outputs:
- hidden: bfloat16 [256, 24576], P('row', 'col')
- grad_input: bfloat16 [256, 12288], P('col', 'row')
- grad_weight: bfloat16 [12288, 24576], P('row', 'col')
- grad_bias: float32 [24576], P('col')
All inputs are finite; a program needn't handle non-finite values.
Results may differ from a plain program's by a relative error of at most 0.0049.
Values may be sent and summed in bfloat16 or wider, within the bound.
A program may use at most 64 MiB of HBM per device.

v0:
```python
import jax
import jax.numpy as jnp
from jax import lax
from jax.sharding import PartitionSpec as P


def gelu_tanh(values):
    return jax.nn.gelu(values, approximate=True)


def gelu_pair(preact, upstream):
    output, pullback = jax.vjp(gelu_tanh, preact)
    return (output, pullback(upstream)[0])


def shards(inputs, weight, hidden_bias, cotangent):
    gathered = lax.all_gather(inputs, "col", axis=0, tiled=True)
    block = gathered
    preact = (
        lax.psum_scatter(
            jnp.dot(block, weight, preferred_element_type=jnp.float32),
            "row",
            scatter_dimension=0,
            tiled=True,
        )
        + hidden_bias
    )
    output, slope = gelu_pair(preact, cotangent.astype(jnp.float32))
    hidden = output.astype(jnp.bfloat16)
    grad_pre = lax.all_gather(slope.astype(jnp.bfloat16), "row", axis=0, tiled=True)
    panels = lax.all_gather(inputs, "col", axis=0, tiled=True)
    grad_weight = lax.dot_general(
        panels, grad_pre, (((0,), (0,)), ((), ())), preferred_element_type=jnp.float32
    ).astype(jnp.bfloat16)
    ones_row = jnp.ones((1, grad_pre.shape[0]), jnp.bfloat16)
    grad_bias = jnp.dot(ones_row, grad_pre, preferred_element_type=jnp.float32)[0]
    block = grad_pre
    grad_input = lax.psum_scatter(
        lax.dot_general(
            block, weight, (((1,), (1,)), ((), ())), preferred_element_type=jnp.float32
        ),
        "col",
        scatter_dimension=0,
        tiled=True,
    ).astype(jnp.bfloat16)
    return (hidden, grad_input, grad_weight, grad_bias)


def solution(mesh):
    placed = (P("col", "row"), P("row", "col"), P("col"), P("row", "col"))
    return jax.shard_map(
        shards,
        mesh=mesh,
        in_specs=placed,
        out_specs=(P("row", "col"), P("col", "row"), P("row", "col"), P("col")),
        check_vma=False,
    )
```

profile of v0, /device:TPU:1, one launch (start us, length us, event | category | flops | bytes accessed | tf_op | source)
XLA Modules:
  0.0 406.7 jit_solution(2439092005832178605)
XLA Ops:
  7.2 0.0 copy-start
  7.2 0.0 reduce-scatter.3.cloned.1.call-start
  7.2 77.3 %all_gather.7 = bf16[256,768]{1,0:T(8,128)(2,1)S(1)} all-gather(bf16[8,768]{1,0:T(8,128)(2,1)} %param.4), channel_id=1, replica_groups=mesh['row'=16,'col'=32] {'col'}, dimensions={0}, use_global_device_ids=true | all-gather | bytes 405504 | tf_op jit(solution)/shard_map/all_gather | solution.py:17
  84.5 0.0 copy-done
  84.5 0.0 copy-start.1
  84.5 0.0 copy-start.2
  84.5 1.4 fusion.13
  85.9 0.0 reduce-scatter.3.cloned.1.call-update
  85.9 0.0 reduce-scatter.5.cloned.1.call-start
  86.0 69.7 %reduce-scatter.3.cloned.1.call-done = f32[16,768]{1,0:T(8,128)} async-done(((f32[256,768]{1,0:T(8,128)}), f32[16,768]{1,0:T(8,128)}) %reduce-scatter.3.cloned.1.call-update) | async-done | bytes 49168 | tf_op jit(solution)/shard_map/reduce_scatter | solution.py:20
  155.6 0.0 copy-done.1
  155.7 0.0 copy-done.2
  155.7 1.4 fusion.3
  157.1 20.2 %all_gather.8 = bf16[256,768]{1,0:T(8,128)(2,1)S(1)} all-gather(bf16[16,768]{1,0:T(8,128)(2,1)S(1)} %get-tuple-element.8), channel_id=1, replica_groups=mesh['row'=16,'col'=32] {'row'}, dimensions={0}, use_global_device_ids=true | all-gather | bytes 417792 | tf_op jit(solution)/shard_map/all_gather | solution.py:30
  177.3 1.4 fusion.14
  178.7 0.0 reduce-scatter.5.cloned.1.call-update
  178.7 0.5 fusion
  179.2 1.5 copy.8
  180.7 0.8 convolution_reduce_fusion
  181.5 217.0 %reduce-scatter.5.cloned.1.call-done = f32[8,768]{1,0:T(8,128)} async-done(((f32[256,768]{1,0:T(8,128)}), f32[8,768]{1,0:T(8,128)}) %reduce-scatter.5.cloned.1.call-update) | async-done | bytes 24592 | tf_op jit(solution)/shard_map/reduce_scatter | solution.py:38
  398.5 1.3 convert_element_type.21
Async XLA Ops:
  7.2 77.3 %copy-start = (bf16[768,768]{1,0:T(8,128)(2,1)S(1)}, bf16[768,768]{1,0:T(8,128)(2,1)}, u32[]{:S(2)}) copy-start(bf16[768,768]{1,0:T(8,128)(2,1)} %param.5) | copy-start | bytes 3538948
  7.2 148.5 %reduce-scatter.3.cloned.1.call-start = ((), (), s32[]{:S(2)}) async-start(), calls=%async_computation.2 | async-start | bytes 835584 | tf_op jit(solution)/shard_map/reduce_scatter | solution.py:20
  84.5 71.1 %copy-start.1 = (bf16[16,768]{1,0:T(8,128)(2,1)S(1)}, bf16[16,768]{1,0:T(8,128)(2,1)}, u32[]{:S(2)}) copy-start(bf16[16,768]{1,0:T(8,128)(2,1)} %param.7) | copy-start | bytes 73732
  84.5 71.1 %copy-start.2 = (f32[768]{0:T(1024)S(1)}, f32[768]{0:T(1024)}, u32[]{:S(2)}) copy-start(f32[768]{0:T(1024)} %param.6) | copy-start | bytes 9220
  85.9 312.6 %reduce-scatter.5.cloned.1.call-start = ((), (), s32[]{:S(2)}) async-start(), calls=%async_computation.3 | async-start | bytes 811008 | tf_op jit(solution)/shard_map/reduce_scatter | solution.py:38
Sparse Core Ops, SparseCore 0:
  86.0 69.5 reduce-scatter.2
  178.8 219.6 reduce-scatter.4
where the time goes:
time: 411 us; the launch traced here: 407 us
  waiting for transfers between devices  287 us (70%)
  blocking collectives  97.5 us (24%)
  between operations  14.1 us (3%)
    reduce_scatter x1, waiting for transfers between devices, shards(): lax.psum_scatter(lax.dot_general(block, weight, (((1,), (1,)), ((), ())),...  217 us
    all_gather x1, blocking collectives, shards(): gathered = lax.all_gather(inputs, 'col', axis=0, tiled=True)  77.3 us
    reduce_scatter x1, waiting for transfers between devices, shards(): lax.psum_scatter(jnp.dot(block, weight, preferred_element_type=jnp.float3...  69.7 us
    all_gather x1, blocking collectives, shards(): lax.all_gather(slope.astype(jnp.bfloat16), 'row', axis=0, tiled=True)  20.2 us
  transfers between devices with their start and end apart: 2, of which 2 were waited for; matrix products, arithmetic and copies ran while one was open for 1% of the time, Pallas kernels for 0%

commit v1 on v0

v1 whole, which is shorter than its diff:
```python
import jax
import jax.numpy as jnp
from jax import lax
from jax.experimental import pallas as pl
from jax.experimental.pallas import tpu as pltpu
from jax.sharding import PartitionSpec as P

MESH = pl.DeviceIdType.MESH
CORES, XS, ZLO, YS, ZHI = 2, 4, 2, 8, 4
ROWS, COLS = ZLO * XS * CORES, ZHI * YS
BF16, F32 = jnp.bfloat16, jnp.float32

ROW_OFFSETS = [
    (dz, dx, dc)
    for dz, dx in ((1, 2), (0, 2), (1, 1), (1, 3), (0, 1), (0, 3), (1, 0), (0, 0))
    for dc in (1, 0)
    if dz or dx or dc
]
Z_ORDER = (0, 1, 3, 2)
FAR_SIDE = {0: 1, 1: -1, 3: 1, 2: -1}


def gelu_and_slope(v):
    c, a = 0.7978845608028654, 0.044715
    v2 = v * v
    t = jnp.tanh(c * (v + a * (v2 * v)))
    half = 0.5 * (1.0 + t)
    return v * half, half + (0.5 * v) * (1.0 - t * t) * (c * (1.0 + (3.0 * a) * v2))


def kernel(
    x_hbm, w_hbm, b_ref, cot_ref,
    hid_ref, gi_ref, gw_hbm, gb_ref,
    w_v, xg, xn, xt, part, psend, precv, g_v, part2, gw_v,
    raw, raw_in, mid, mid_in, zout, zin,
    local_sem, za_s, za_r, ya_s, ya_r, p_s, p_r, g_s, g_r, e_s, e_r, ez_s, ez_r,
):
    r = lax.axis_index("row")
    c = lax.axis_index("col")
    core, x, zlo = lax.rem(r, 2), lax.rem(lax.div(r, 2), XS), lax.div(r, 8)
    y, z = lax.rem(c, YS), lax.div(c, YS)

    def at_row(dz, dx, dc):
        return (lax.rem(zlo + dz, ZLO) * XS + lax.rem(x + dx, XS)) * CORES + lax.rem(core + dc, CORES)

    def wy(d):
        return lax.rem(y + (d + YS), YS)

    def wz(d):
        return lax.rem(z + (d + ZHI), ZHI)

    def to_row(o):
        return {"row": at_row(*o), "col": c}

    def to_y(d):
        return {"row": r, "col": z * YS + wy(d)}

    def to_z(d):
        return {"row": r, "col": wz(d) * YS + y}

    def send(src, dst, s, q, dev):
        return pltpu.make_async_remote_copy(
            src_ref=src, dst_ref=dst, send_sem=s, recv_sem=q, device_id=dev, device_id_type=MESH
        )

    peers = [to_y(d) for d in (1, -1, 2, -2)] + [to_z(d) for d in (1, 2, 3)] + [to_row(o) for o in ROW_OFFSETS]
    barrier = pltpu.get_barrier_semaphore()
    for dev in peers:
        pl.semaphore_signal(barrier, inc=1, device_id=dev, device_id_type=MESH)
    x_in = pltpu.make_async_copy(x_hbm, xg.at[y, z], local_sem.at[0])
    w_in = pltpu.make_async_copy(w_hbm, w_v, local_sem.at[1])
    x_in.start()
    w_in.start()
    x_in.wait()
    pl.semaphore_wait(barrier, len(peers))

    pending = []
    zc = {}
    for d in (2, 1, 3):
        zc[d] = send(xg.at[y, z], xg.at[y, z], za_s.at[d], za_r.at[d], to_z(d))
        zc[d].start()
        pending.append(zc[d])
    near = {}
    for k in Z_ORDER:
        zk = wz(-k)
        if k:
            zc[k].wait_recv()
        for i, d in enumerate((2, -2, 1, -1)):
            block = xg.at[y, zk]
            near[k, d] = send(block, block, ya_s.at[k, i], ya_r.at[k, i], to_y(d))
            near[k, d].start()
            pending.append(near[k, d])
    far = []
    for k in Z_ORDER:
        zk = wz(-k)
        for i, side in enumerate((1, -1)):
            near[k, 2 * side].wait_recv()
            block = xg.at[wy(-2 * side), zk]
            if FAR_SIDE[k] == side:
                far.append(send(block, block, ya_s.at[k, 4], ya_r.at[k, 4], to_y(2 * side)))
                far[-1].start()
            far.append(send(block, block, ya_s.at[k, 5 + i], ya_r.at[k, 5 + i], to_y(side)))
            far[-1].start()
    pending += far
    w_in.wait()
    for k in Z_ORDER:
        near[k, 1].wait_recv()
        near[k, -1].wait_recv()
    for cp in far:
        cp.wait_recv()

    for rr in range(ROWS):
        zz, yy = rr // 4, 2 * (rr % 4)
        pair = jnp.concatenate([xg[yy, zz].astype(F32), xg[yy + 1, zz].astype(F32)], axis=0)
        xn[pl.ds(16 * rr, 16), :] = pair.astype(BF16)
    part[...] = jnp.dot(xn[...], w_v[...], preferred_element_type=F32)

    sums = []
    for i, o in enumerate(ROW_OFFSETS):
        rows = pl.ds(pl.multiple_of(at_row(*o) * 16, 16), 16)
        psend[i] = part[rows, :].astype(BF16)
        sums.append(send(psend.at[i], precv.at[i], p_s.at[i], p_r.at[i], to_row(o)))
        sums[-1].start()
    pending += sums
    mine = pl.ds(pl.multiple_of(r * 16, 16), 16)
    v = part[mine, :] + b_ref[...].reshape(1, -1)
    xt[...] = xn[...].T
    for i in reversed(range(len(ROW_OFFSETS))):
        sums[i].wait_recv()
        v = v + precv[i].astype(F32)

    hidden, slope = gelu_and_slope(v)
    g_v[mine, :] = (cot_ref[...].astype(F32) * slope).astype(BF16)

    grads = []
    for i, o in enumerate(ROW_OFFSETS):
        grads.append(send(g_v.at[mine, :], g_v.at[mine, :], g_s.at[i], g_r.at[i], to_row(o)))
        grads[-1].start()
    pending += grads
    hid_ref[...] = hidden.astype(BF16)
    for cp in grads:
        cp.wait_recv()

    part2[...] = lax.dot_general(g_v[...], w_v[...], (((1,), (1,)), ((), ())), preferred_element_type=F32)

    def share(d, zk):
        return part2[pl.ds(pl.multiple_of((zk * YS + wy(d)) * 8, 8), 8), :]

    order = (2, 1, 3, 0)
    legs = {}
    for k in order:
        zk = wz(k)
        side = FAR_SIDE[k]
        for j, final, via in ((0, 4, 2 * side), (1, 3, 1), (2, -3, -1), (3, 1, 1), (4, -1, -1)):
            raw[k, j] = share(final, zk).astype(BF16)
            legs[k, j] = send(raw.at[k, j], raw_in.at[k, j], e_s.at[k, j], e_r.at[k, j], to_y(via))
            legs[k, j].start()
            pending.append(legs[k, j])

    gw_v[...] = jnp.dot(xt[...], g_v[...], preferred_element_type=F32).astype(BF16)
    gw_out = pltpu.make_async_copy(gw_v, gw_hbm, local_sem.at[0])
    gw_out.start()
    gb_ref[...] = jnp.sum(g_v[...].astype(F32), axis=0)

    for k in order:
        zk = wz(k)
        legs[k, 0].wait_recv()
        for j, side in ((0, 1), (1, -1)):
            legs[k, 1 + j].wait_recv()
            s = share(2 * side, zk) + raw_in[k, 1 + j].astype(F32)
            if FAR_SIDE[k] == side:
                s = s + raw_in[k, 0].astype(F32)
            mid[k, j] = s.astype(BF16)
            legs[k, 5 + j] = send(mid.at[k, j], mid_in.at[k, j], e_s.at[k, 5 + j], e_r.at[k, 5 + j], to_y(2 * side))
            legs[k, 5 + j].start()
            pending.append(legs[k, 5 + j])
    last = {}
    for k in order:
        zk = wz(k)
        s = share(0, zk)
        for j in (3, 4):
            legs[k, j].wait_recv()
            s = s + raw_in[k, j].astype(F32)
        for j in (0, 1):
            legs[k, 5 + j].wait_recv()
            s = s + mid_in[k, j].astype(F32)
        if k:
            zout[k] = s
            last[k] = send(zout.at[k], zin.at[k], ez_s.at[k], ez_r.at[k], to_z(k))
            last[k].start()
            pending.append(last[k])
    for k in (1, 3, 2):
        last[k].wait_recv()
        s = s + zin[k]
    gi_ref[...] = s.astype(BF16)
    for cp in pending:
        cp.wait_send()
    gw_out.wait()


def shards(inputs, weight, hidden_bias, cotangent):
    tok, feat = inputs.shape
    hid = weight.shape[1]
    all_tok = tok * COLS
    vmem = pl.BlockSpec(memory_space=pltpu.VMEM)
    hbm = pl.BlockSpec(memory_space=pl.ANY)
    dma = pltpu.SemaphoreType.DMA
    n_row = len(ROW_OFFSETS)
    return pl.pallas_call(
        kernel,
        out_shape=(
            jax.ShapeDtypeStruct(cotangent.shape, BF16),
            jax.ShapeDtypeStruct(inputs.shape, BF16),
            jax.ShapeDtypeStruct(weight.shape, BF16),
            jax.ShapeDtypeStruct(hidden_bias.shape, F32),
        ),
        in_specs=[hbm, hbm, vmem, vmem],
        out_specs=(vmem, vmem, hbm, vmem),
        scratch_shapes=[
            pltpu.VMEM((feat, hid), BF16),
            pltpu.VMEM((YS, ZHI, tok, feat), BF16),
            pltpu.VMEM((all_tok, feat), BF16),
            pltpu.VMEM((feat, all_tok), BF16),
            pltpu.VMEM((all_tok, hid), F32),
            pltpu.VMEM((n_row, 16, hid), BF16),
            pltpu.VMEM((n_row, 16, hid), BF16),
            pltpu.VMEM((all_tok, hid), BF16),
            pltpu.VMEM((all_tok, feat), F32),
            pltpu.VMEM((feat, hid), BF16),
            pltpu.VMEM((ZHI, 5, tok, feat), BF16),
            pltpu.VMEM((ZHI, 5, tok, feat), BF16),
            pltpu.VMEM((ZHI, 2, tok, feat), BF16),
            pltpu.VMEM((ZHI, 2, tok, feat), BF16),
            pltpu.VMEM((ZHI, tok, feat), F32),
            pltpu.VMEM((ZHI, tok, feat), F32),
            dma((2,)),
            dma((ZHI,)),
            dma((ZHI,)),
            dma((ZHI, 7)),
            dma((ZHI, 7)),
            dma((n_row,)),
            dma((n_row,)),
            dma((n_row,)),
            dma((n_row,)),
            dma((ZHI, 7)),
            dma((ZHI, 7)),
            dma((ZHI,)),
            dma((ZHI,)),
        ],
        compiler_params=pltpu.CompilerParams(
            collective_id=0, has_side_effects=True, vmem_limit_bytes=32 * 1024 * 1024
        ),
    )(inputs, weight, hidden_bias, cotangent)


def solution(mesh):
    placed = (P("col", "row"), P("row", "col"), P("col"), P("row", "col"))
    return jax.shard_map(
        shards,
        mesh=mesh,
        in_specs=placed,
        out_specs=(P("row", "col"), P("col", "row"), P("row", "col"), P("col")),
        check_vma=False,
    )
```

time: 411 us -> 61.4 us (0.15)
  the two profiles are of different devices: /device:TPU:1 before, /device:TPU:6 now
where the time goes in v1:
time: 61.4 us; the launch traced here: 61.1 us
  Pallas kernels  54.2 us (88%)
  local copies, waits for them, and re-layouts  6.21 us (10%)
  between operations  0.65 us (1%)
    pallas_call x1, Pallas kernels, shards(): pl.pallas_call(kernel, out_shape=(jax.ShapeDtypeStruct(cotangent.shape, B...  54.2 us
    unnamed x12, local copies, waits for them, and re-layouts  6.21 us

profile of v1, /device:TPU:6, one launch (start us, length us, event | category | flops | bytes accessed | tf_op | source)
XLA Modules:
  0.0 61.1 jit_solution(6683053712648052368)
XLA Ops:
  0.6 0.0 copy-start
  0.6 1.3 %copy-done = bf16[768,768]{1,0:T(8,128)(2,1)S(1)} copy-done((bf16[768,768]{1,0:T(8,128)(2,1)S(1)}, bf16[768,768]{1,0:T(8,128)(2,1)}, u32[]{:S(2)}) %copy-start) | copy-done | bytes 1179672
  1.9 0.0 copy-start.1
  1.9 0.7 %copy-done.1 = bf16[16,768]{1,0:T(8,128)(2,1)S(1)} copy-done((bf16[16,768]{1,0:T(8,128)(2,1)S(1)}, bf16[16,768]{1,0:T(8,128)(2,1)}, u32[]{:S(2)}) %copy-start.1) | copy-done | bytes 24600
  2.6 0.0 copy-start.2
  2.6 0.7 %copy-done.2 = bf16[8,768]{1,0:T(8,128)(2,1)S(1)} copy-done((bf16[8,768]{1,0:T(8,128)(2,1)S(1)}, bf16[8,768]{1,0:T(8,128)(2,1)}, u32[]{:S(2)}) %copy-start.2) | copy-done | bytes 12312
  3.3 0.0 copy-start.3
  3.4 0.7 %copy-done.3 = f32[768]{0:T(1024)S(1)} copy-done((f32[768]{0:T(1024)S(1)}, f32[768]{0:T(1024)}, u32[]{:S(2)}) %copy-start.3) | copy-done | bytes 3096
  4.0 54.2 %shard_map.75 = (bf16[16,768]{1,0:T(8,128)(2,1)S(1)}, bf16[8,768]{1,0:T(8,128)(2,1)S(1)}, bf16[768,768]{1,0:T(8,128)(2,1)S(1)}, f32[768]{0:T(1024)S(1)}) custom-call(bf16[8,768]{1,0:T(8,128)(2,1)S(1)} %copy-done.2, bf16[768,768]{1,0:T(8,128)(2,1)S(1)} %copy-done, f32[768]{0:T(1024)S(1)} %copy-done.3, bf16[16,768]{1,0:T(8,128)(2,1)S(1)} %copy-done.1), custom_call_target="tpu_custom_call" | custom-call | tf_op jit(solution)/shard_map/pallas_call | solution.py:209
  58.3 0.6 copy.12
  58.9 0.6 copy.13
  59.5 1.0 %copy.14 = bf16[768,768]{1,0:T(8,128)(2,1)} copy(bf16[768,768]{1,0:T(8,128)(2,1)S(1)} %get-tuple-element.10) | data formatting | bytes 2359296
  60.5 0.6 copy.15
Async XLA Ops:
  0.6 1.3 %copy-start = (bf16[768,768]{1,0:T(8,128)(2,1)S(1)}, bf16[768,768]{1,0:T(8,128)(2,1)}, u32[]{:S(2)}) copy-start(bf16[768,768]{1,0:T(8,128)(2,1)} %w_hbm.1) | copy-start | bytes 3538948
  1.9 0.7 %copy-start.1 = (bf16[16,768]{1,0:T(8,128)(2,1)S(1)}, bf16[16,768]{1,0:T(8,128)(2,1)}, u32[]{:S(2)}) copy-start(bf16[16,768]{1,0:T(8,128)(2,1)} %cot_ref.1) | copy-start | bytes 73732
  2.6 0.7 %copy-start.2 = (bf16[8,768]{1,0:T(8,128)(2,1)S(1)}, bf16[8,768]{1,0:T(8,128)(2,1)}, u32[]{:S(2)}) copy-start(bf16[8,768]{1,0:T(8,128)(2,1)} %x_hbm.1) | copy-start | bytes 36868
  3.3 0.7 %copy-start.3 = (f32[768]{0:T(1024)S(1)}, f32[768]{0:T(1024)}, u32[]{:S(2)}) copy-start(f32[768]{0:T(1024)} %b_ref.1) | copy-start | bytes 9220

commit v2 on v1

v2 whole, which is shorter than its diff:
```python
import jax
import jax.numpy as jnp
from jax import lax
from jax.experimental import pallas as pl
from jax.experimental.pallas import tpu as pltpu
from jax.sharding import PartitionSpec as P

MESH = pl.DeviceIdType.MESH
CORES, XS, ZLO, YS, ZHI = 2, 4, 2, 8, 4
ROWS, COLS = ZLO * XS * CORES, ZHI * YS
BF16, F32 = jnp.bfloat16, jnp.float32

ROW_OFFSETS = [
    (dz, dx, dc)
    for dz, dx in ((1, 2), (0, 2), (1, 1), (1, 3), (0, 1), (0, 3), (1, 0), (0, 0))
    for dc in (1, 0)
    if dz or dx or dc
]
CHIPS = [(1, 2), (1, 1), (1, 3), (0, 2), (1, 0), (0, 1), (0, 3)]
Z_ORDER = (0, 1, 3, 2)
FAR_SIDE = {0: 1, 1: -1, 3: 1, 2: -1}


def gelu_and_slope(v):
    c, a = 0.7978845608028654, 0.044715
    v2 = v * v
    t = jnp.tanh(c * (v + a * (v2 * v)))
    half = 0.5 * (1.0 + t)
    return v * half, half + (0.5 * v) * (1.0 - t * t) * (c * (1.0 + (3.0 * a) * v2))


def kernel(
    x_hbm, w_hbm, b_ref, cot_ref,
    hid_ref, gi_ref, gw_ref, gb_ref,
    w_v, xg, xn, xt, own, psend, precv, g_v, part2,
    raw, raw_in, mid, mid_in, zout, zin,
    local_sem, za_s, za_r, ya_s, ya_r, p_s, p_r, g_s, g_r, h_s, h_r, e_s, e_r, ez_s, ez_r,
):
    r = lax.axis_index("row")
    c = lax.axis_index("col")
    core, x, zlo = lax.rem(r, 2), lax.rem(lax.div(r, 2), XS), lax.div(r, 8)
    y, z = lax.rem(c, YS), lax.div(c, YS)

    def at_row(dz, dx, dc):
        return (lax.rem(zlo + dz, ZLO) * XS + lax.rem(x + dx, XS)) * CORES + lax.rem(core + dc, CORES)

    def wy(d):
        return lax.rem(y + (d + YS), YS)

    def wz(d):
        return lax.rem(z + (d + ZHI), ZHI)

    def to_row(o):
        return {"row": at_row(*o), "col": c}

    def to_y(d):
        return {"row": r, "col": z * YS + wy(d)}

    def to_z(d):
        return {"row": r, "col": wz(d) * YS + y}

    def send(src, dst, s, q, dev):
        return pltpu.make_async_remote_copy(
            src_ref=src, dst_ref=dst, send_sem=s, recv_sem=q, device_id=dev, device_id_type=MESH
        )

    peers = [to_y(d) for d in (1, -1, 2, -2)] + [to_z(d) for d in (1, 2, 3)] + [to_row(o) for o in ROW_OFFSETS]
    barrier = pltpu.get_barrier_semaphore()
    for dev in peers:
        pl.semaphore_signal(barrier, inc=1, device_id=dev, device_id_type=MESH)
    x_in = pltpu.make_async_copy(x_hbm, xg.at[y, z], local_sem.at[0])
    w_in = pltpu.make_async_copy(w_hbm, w_v, local_sem.at[1])
    x_in.start()
    w_in.start()
    x_in.wait()
    pl.semaphore_wait(barrier, len(peers))

    pending = []
    zc, near = {}, {}
    far = {k: [] for k in Z_ORDER}

    def forward_near(k):
        for i, d in enumerate((2, -2, 1, -1)):
            block = xg.at[y, wz(-k)]
            near[k, d] = send(block, block, ya_s.at[k, i], ya_r.at[k, i], to_y(d))
            near[k, d].start()
            pending.append(near[k, d])

    def forward_far(k):
        for i, side in enumerate((1, -1)):
            near[k, 2 * side].wait_recv()
            block = xg.at[wy(-2 * side), wz(-k)]
            if FAR_SIDE[k] == side:
                far[k].append(send(block, block, ya_s.at[k, 4], ya_r.at[k, 4], to_y(2 * side)))
                far[k][-1].start()
            far[k].append(send(block, block, ya_s.at[k, 5 + i], ya_r.at[k, 5 + i], to_y(side)))
            far[k][-1].start()
        pending.extend(far[k])

    def multiply(k):
        zk = wz(-k)
        for cp in [near[k, 1], near[k, -1]] + far[k]:
            cp.wait_recv()
        rows = pl.ds(pl.multiple_of(zk * 64, 64), 64)
        xs = jnp.concatenate([xg[yy, zk].astype(F32) for yy in range(YS)], axis=0).astype(BF16)
        xn[rows, :] = xs
        share = jnp.dot(xs, w_v[...], preferred_element_type=F32)
        for j in range(4):
            owner = zk * 4 + j
            d = lax.rem(owner - r + ROWS, ROWS)
            part = share[16 * j : 16 * j + 16, :]
            psend[4 * k + j] = part.astype(BF16)

            @pl.when(d != 0)
            def _():
                send(psend.at[4 * k + j], precv.at[d], p_s.at[d], p_r.at[d], {"row": owner, "col": c}).start()

            @pl.when(d == 0)
            def _():
                own[...] = part

    for d in (2, 1, 3):
        zc[d] = send(xg.at[y, z], xg.at[y, z], za_s.at[d], za_r.at[d], to_z(d))
        zc[d].start()
        pending.append(zc[d])
    forward_near(0)
    for k in (1, 3):
        zc[k].wait_recv()
        forward_near(k)
    forward_far(0)
    zc[2].wait_recv()
    forward_near(2)
    w_in.wait()
    forward_far(1)
    forward_far(3)
    multiply(0)
    forward_far(2)
    for k in (1, 3, 2):
        multiply(k)

    xt[...] = xn[...].T
    v = own[...] + b_ref[...].reshape(1, -1)
    for d in range(1, ROWS):
        cp = send(psend.at[d], precv.at[d], p_s.at[d], p_r.at[d], to_row(ROW_OFFSETS[0]))
        cp.wait_recv()
        pending.append(cp)
        v = v + precv[d].astype(F32)

    mine = pl.ds(pl.multiple_of(r * 16, 16), 16)
    hidden, slope = gelu_and_slope(v)
    g_v[mine, :] = (cot_ref[...].astype(F32) * slope).astype(BF16)

    other = {"row": at_row(0, 0, 1), "col": c}
    grads, passed = [], []
    for i, (dz, dx) in enumerate(CHIPS):
        grads.append(send(g_v.at[mine, :], g_v.at[mine, :], g_s.at[i], g_r.at[i], to_row((dz, dx, 0))))
        grads[-1].start()

    def hand_over(i, rows):
        passed.append(send(g_v.at[rows, :], g_v.at[rows, :], h_s.at[i], h_r.at[i], other))
        passed[-1].start()

    hand_over(len(CHIPS), mine)
    hid_ref[...] = hidden.astype(BF16)
    for i in reversed(range(len(CHIPS))):
        dz, dx = CHIPS[i]
        grads[i].wait_recv()
        hand_over(i, pl.ds(pl.multiple_of(at_row(ZLO - dz, XS - dx, 0) * 16, 16), 16))
    for cp in passed:
        cp.wait_recv()
    pending += grads + passed

    legs = {}

    def share(d, zk):
        return part2[pl.ds(pl.multiple_of((zk * YS + wy(d)) * 8, 8), 8), :]

    def leave(k, j, src, dst, d):
        legs[k, j] = send(src, dst, e_s.at[k, j], e_r.at[k, j], to_y(d))
        legs[k, j].start()
        pending.append(legs[k, j])

    def first_legs(k, which):
        zk = wz(k)
        for j, final, via in which:
            raw[k, j] = share(final, zk).astype(BF16)
            leave(k, j, raw.at[k, j], raw_in.at[k, j], via(k))

    def second_legs(k):
        zk = wz(k)
        legs[k, 0].wait_recv()
        for j, side in ((0, 1), (1, -1)):
            legs[k, 1 + j].wait_recv()
            s = share(2 * side, zk) + raw_in[k, 1 + j].astype(F32)
            if FAR_SIDE[k] == side:
                s = s + raw_in[k, 0].astype(F32)
            mid[k, j] = s.astype(BF16)
            leave(k, 5 + j, mid.at[k, j], mid_in.at[k, j], 2 * side)

    def y_total(k):
        s = share(0, wz(k))
        for j in (3, 4):
            legs[k, j].wait_recv()
            s = s + raw_in[k, j].astype(F32)
        for j in (0, 1):
            legs[k, 5 + j].wait_recv()
            s = s + mid_in[k, j].astype(F32)
        return s

    last = {}

    def z_leg(k):
        zout[k] = y_total(k).astype(BF16)
        last[k] = send(zout.at[k], zin.at[k], ez_s.at[k], ez_r.at[k], to_z(k))
        last[k].start()
        pending.append(last[k])

    part2[...] = lax.dot_general(g_v[...], w_v[...], (((1,), (1,)), ((), ())), preferred_element_type=F32)
    order = (2, 1, 3, 0)
    for k in order:
        first_legs(k, ((0, 4, lambda k: 2 * FAR_SIDE[k]), (1, 3, lambda k: 1), (2, -3, lambda k: -1)))
    for k in order:
        first_legs(k, ((3, 1, lambda k: 1), (4, -1, lambda k: -1)))
    gw_ref[...] = jnp.dot(xt[...], g_v[...], preferred_element_type=F32).astype(BF16)
    gb_ref[...] = jnp.sum(g_v[...].astype(F32), axis=0)
    for k in order:
        second_legs(k)
    z_leg(2)
    z_leg(1)
    z_leg(3)
    s = y_total(0)
    for k in (1, 3, 2):
        last[k].wait_recv()
        s = s + zin[k].astype(F32)
    gi_ref[...] = s.astype(BF16)
    for cp in pending:
        cp.wait_send()


def store(*refs):
    sem = refs[8]
    copies = [pltpu.make_async_copy(refs[i], refs[4 + i], sem.at[i]) for i in range(4)]
    for cp in copies:
        cp.start()
    for cp in copies:
        cp.wait()


def shards(inputs, weight, hidden_bias, cotangent):
    tok, feat = inputs.shape
    hid = weight.shape[1]
    all_tok = tok * COLS
    vmem = pl.BlockSpec(memory_space=pltpu.VMEM)
    hbm = pl.BlockSpec(memory_space=pl.ANY)
    dma = pltpu.SemaphoreType.DMA
    outs = pl.pallas_call(
        kernel,
        out_shape=(
            pltpu.VMEM(cotangent.shape, BF16),
            pltpu.VMEM(inputs.shape, BF16),
            pltpu.VMEM(weight.shape, BF16),
            pltpu.VMEM(hidden_bias.shape, F32),
        ),
        in_specs=[hbm, hbm, vmem, vmem],
        out_specs=(vmem, vmem, vmem, vmem),
        scratch_shapes=[
            pltpu.VMEM((feat, hid), BF16),
            pltpu.VMEM((YS, ZHI, tok, feat), BF16),
            pltpu.VMEM((all_tok, feat), BF16),
            pltpu.VMEM((feat, all_tok), BF16),
            pltpu.VMEM((16, hid), F32),
            pltpu.VMEM((ROWS, 16, hid), BF16),
            pltpu.VMEM((ROWS, 16, hid), BF16),
            pltpu.VMEM((all_tok, hid), BF16),
            pltpu.VMEM((all_tok, feat), F32),
            pltpu.VMEM((ZHI, 5, tok, feat), BF16),
            pltpu.VMEM((ZHI, 5, tok, feat), BF16),
            pltpu.VMEM((ZHI, 2, tok, feat), BF16),
            pltpu.VMEM((ZHI, 2, tok, feat), BF16),
            pltpu.VMEM((ZHI, tok, feat), BF16),
            pltpu.VMEM((ZHI, tok, feat), BF16),
            dma((2,)),
            dma((ZHI,)),
            dma((ZHI,)),
            dma((ZHI, 7)),
            dma((ZHI, 7)),
            dma((ROWS,)),
            dma((ROWS,)),
            dma((len(CHIPS),)),
            dma((len(CHIPS),)),
            dma((len(CHIPS) + 1,)),
            dma((len(CHIPS) + 1,)),
            dma((ZHI, 7)),
            dma((ZHI, 7)),
            dma((ZHI,)),
            dma((ZHI,)),
        ],
        compiler_params=pltpu.CompilerParams(
            collective_id=0, has_side_effects=True, vmem_limit_bytes=32 * 1024 * 1024
        ),
    )(*(pltpu.with_memory_space_constraint(a, pltpu.HBM) for a in (inputs, weight, hidden_bias, cotangent)))
    return pl.pallas_call(
        store,
        out_shape=[pltpu.HBM(o.shape, o.dtype) for o in outs],
        in_specs=[vmem] * 4,
        out_specs=[hbm] * 4,
        scratch_shapes=[dma((4,))],
    )(*(pltpu.with_memory_space_constraint(o, pltpu.VMEM) for o in outs))


def solution(mesh):
    placed = (P("col", "row"), P("row", "col"), P("col"), P("row", "col"))
    return jax.shard_map(
        shards,
        mesh=mesh,
        in_specs=placed,
        out_specs=(P("row", "col"), P("col", "row"), P("row", "col"), P("col")),
        check_vma=False,
    )
```

time: 61.4 us -> 54.5 us (0.89)
  the two profiles are of different devices: /device:TPU:6 before, /device:TPU:72 now
where the time goes in v2:
time: 54.5 us; the launch traced here: 54.3 us
  Pallas kernels  53.6 us (98%)
  between operations  0.64 us (1%)
    pallas_call x1, Pallas kernels, shards(): pl.pallas_call(kernel, out_shape=(pltpu.VMEM(cotangent.shape, BF16), pltp...  52.6 us

profile of v2, /device:TPU:72, one launch (start us, length us, event | category | flops | bytes accessed | tf_op | source)
XLA Modules:
  0.0 54.3 jit_solution(12957925000335267130)
XLA Ops:
  0.6 52.6 %shard_map.75 = (bf16[16,768]{1,0:T(8,128)(2,1)S(1)}, bf16[8,768]{1,0:T(8,128)(2,1)S(1)}, bf16[768,768]{1,0:T(8,128)(2,1)S(1)}, f32[768]{0:T(1024)S(1)}) custom-call(bf16[8,768]{1,0:T(8,128)(2,1)} %x_hbm.1, bf16[768,768]{1,0:T(8,128)(2,1)} %w_hbm.1, f32[768]{0:T(1024)} %b_ref.1, bf16[16,768]{1,0:T(8,128)(2,1)} %cot_ref.1), custom_call_target="tpu_custom_call" | custom-call | tf_op jit(solution)/shard_map/pallas_call | solution.py:256
  53.2 1.1 %shard_map.76 = (bf16[16,768]{1,0:T(8,128)(2,1)}, bf16[8,768]{1,0:T(8,128)(2,1)}, bf16[768,768]{1,0:T(8,128)(2,1)}, f32[768]{0:T(1024)}) custom-call(bf16[16,768]{1,0:T(8,128)(2,1)S(1)} %get-tuple-element.8.refs_0_, bf16[8,768]{1,0:T(8,128)(2,1)S(1)} %get-tuple-element.9.refs_1_, bf16[768,768]{1,0:T(8,128)(2,1)S(1)} %get-tuple-element.10.refs_2_, ...), custom_call_target="tpu_custom_call" | custom-call | tf_op jit(solution)/shard_map/pallas_call | solution.py:302

commit v3 on v2

v3 whole, which is shorter than its diff:
```python
import jax
import jax.numpy as jnp
from jax import lax
from jax.experimental import pallas as pl
from jax.experimental.pallas import tpu as pltpu
from jax.sharding import PartitionSpec as P

MESH = pl.DeviceIdType.MESH
CORES, XS, ZLO, YS, ZHI = 2, 4, 2, 8, 4
ROWS, COLS = ZLO * XS * CORES, ZHI * YS
BF16, F32 = jnp.bfloat16, jnp.float32

CHIPS = [(1, 2), (1, 1), (1, 3), (0, 2), (1, 0), (0, 1), (0, 3)]
NEAR, FAR = (2, -2, 1, -1), (4, 3, -3)
Z_OFFSETS = (2, 1, 3)


def gelu_and_slope(v):
    c, a = 0.7978845608028654, 0.044715
    v2 = v * v
    t = jnp.tanh(c * (v + a * (v2 * v)))
    half = 0.5 * (1.0 + t)
    return v * half, half + (0.5 * v) * (1.0 - t * t) * (c * (1.0 + (3.0 * a) * v2))


def kernel(
    x_hbm, w_hbm, b_ref, cot_ref,
    hid_ref, gi_ref, gw_ref, gb_ref,
    w_v, xg, xn, xt, mine_f, own, csend, crecv, psend, precv, g_v, part2,
    y1_out, y1_in, z1_out, z1_in, y2_out, y2_in, z2_out, z2_in,
    local_sem, a_s, a_r, c_s, c_r, p_s, p_r, g_s, g_r, h_s, h_r,
    y1_s, y1_r, z1_s, z1_r, y2_s, y2_r, z2_s, z2_r,
):
    r = lax.axis_index("row")
    c = lax.axis_index("col")
    core, x, zlo = lax.rem(r, 2), lax.rem(lax.div(r, 2), XS), lax.div(r, 8)
    y, z = lax.rem(c, YS), lax.div(c, YS)

    def at_row(dz, dx, dc):
        return (lax.rem(zlo + dz, ZLO) * XS + lax.rem(x + dx, XS)) * CORES + lax.rem(core + dc, CORES)

    def wy(d):
        return lax.rem(y + (d + YS), YS)

    def wz(d):
        return lax.rem(z + (d + ZHI), ZHI)

    def to_chip(dz, dx):
        return {"row": at_row(dz, dx, 0), "col": c}

    def to_y(d):
        return {"row": r, "col": z * YS + wy(d)}

    def to_z(d):
        return {"row": r, "col": wz(d) * YS + y}

    other = {"row": at_row(0, 0, 1), "col": c}
    pending = []

    def send(src, dst, s, q, dev):
        cp = pltpu.make_async_remote_copy(
            src_ref=src, dst_ref=dst, send_sem=s, recv_sem=q, device_id=dev, device_id_type=MESH
        )
        cp.start()
        pending.append(cp)
        return cp

    peers = [to_z(d) for d in Z_OFFSETS] + [to_y(d) for d in FAR + NEAR] + [to_chip(*o) for o in CHIPS] + [other]
    barrier = pltpu.get_barrier_semaphore()
    for dev in peers:
        pl.semaphore_signal(barrier, inc=1, device_id=dev, device_id_type=MESH)
    x_in = pltpu.make_async_copy(x_hbm, xg.at[y, z], local_sem.at[0])
    w_in = pltpu.make_async_copy(w_hbm, w_v, local_sem.at[1])
    x_in.start()
    w_in.start()
    x_in.wait()
    pl.semaphore_wait(barrier, len(peers))

    blocks = {}

    def pass_on(k, d, hop_k, hop_d):
        block = xg.at[wy(-d), wz(-k)]
        key = k + hop_k, d + hop_d
        at = key[0], key[1] % YS
        blocks[key] = send(block, block, a_s.at[at], a_r.at[at], to_z(hop_k) if hop_k else to_y(hop_d))

    for d in FAR:
        pass_on(0, 0, 0, d)
    for k in Z_OFFSETS:
        pass_on(0, 0, k, 0)
    for d in NEAR:
        pass_on(0, 0, 0, d)
    for k, d in ((1, 0), (3, 0), (0, 3), (0, -3), (2, 0), (0, 4)):
        blocks[k, d].wait_recv()
        if k:
            for hop in NEAR:
                pass_on(k, d, 0, hop)
        else:
            for hop in Z_OFFSETS:
                pass_on(k, d, hop, 0)

    halves = {}

    def multiply(k):
        zk = wz(-k)
        for d in NEAR + (FAR if k else ()):
            blocks[k, d].wait_recv()
        rows = pl.ds(pl.multiple_of(zk * 64, 64), 64)
        xs = jnp.concatenate([xg[yy, zk].astype(F32) for yy in range(YS)], axis=0).astype(BF16)
        xn[rows, :] = xs
        psend_f = jnp.dot(xs, w_v[...], preferred_element_type=F32)
        for j in range(2):
            for cc in range(2):
                part = psend_f[32 * j + 16 * cc : 32 * j + 16 * cc + 16, :]

                @pl.when(core == cc)
                def _():
                    own[k, j] = part

                @pl.when(core != cc)
                def _():
                    csend[k, j] = part

        halves[k] = send(csend.at[k], crecv.at[k], c_s.at[k], c_r.at[k], other)

    def to_owners(k):
        zk = wz(-k)
        halves[k].wait_recv()
        for j in range(2):
            chip = zk * 2 + j
            d = lax.rem(chip - lax.div(r, 2) + 8, 8)
            part = own[k, j] + crecv[k, j]
            psend[k, j] = part.astype(BF16)

            @pl.when(d != 0)
            def _():
                pltpu.make_async_remote_copy(
                    src_ref=psend.at[k, j], dst_ref=precv.at[d], send_sem=p_s.at[d], recv_sem=p_r.at[d],
                    device_id={"row": chip * 2 + core, "col": c}, device_id_type=MESH,
                ).start()

            @pl.when(d == 0)
            def _():
                mine_f[...] = part

    w_in.wait()
    multiply(0)
    to_owners(0)
    multiply(1)
    multiply(3)
    to_owners(1)
    to_owners(3)
    multiply(2)
    to_owners(2)

    xt[...] = xn[...].T
    v = mine_f[...] + b_ref[...].reshape(1, -1)
    for d in range(1, 8):
        cp = pltpu.make_async_remote_copy(
            src_ref=psend.at[d // 2, d % 2], dst_ref=precv.at[d], send_sem=p_s.at[d], recv_sem=p_r.at[d],
            device_id=other, device_id_type=MESH,
        )
        cp.wait_recv()
        pending.append(cp)
        v = v + precv[d].astype(F32)

    mine = pl.ds(pl.multiple_of(r * 16, 16), 16)
    hidden, slope = gelu_and_slope(v)
    g_v[mine, :] = (cot_ref[...].astype(F32) * slope).astype(BF16)

    grads, passed = [], []
    for i, (dz, dx) in enumerate(CHIPS):
        grads.append(send(g_v.at[mine, :], g_v.at[mine, :], g_s.at[i], g_r.at[i], to_chip(dz, dx)))

    def hand_over(i, rows):
        passed.append(send(g_v.at[rows, :], g_v.at[rows, :], h_s.at[i], h_r.at[i], other))

    hand_over(len(CHIPS), mine)
    hid_ref[...] = hidden.astype(BF16)
    for i in reversed(range(len(CHIPS))):
        dz, dx = CHIPS[i]
        grads[i].wait_recv()
        hand_over(i, pl.ds(pl.multiple_of(at_row(ZLO - dz, XS - dx, 0) * 16, 16), 16))
    for cp in passed:
        cp.wait_recv()

    part2[...] = lax.dot_general(g_v[...], w_v[...], (((1,), (1,)), ((), ())), preferred_element_type=F32)

    def share(k, d):
        return part2[pl.ds(pl.multiple_of((wz(k) * YS + wy(d)) * 8, 8), 8), :]

    z1, y1, z2, y2 = {}, {}, {}, {}
    for k in Z_OFFSETS:
        for i, d in enumerate(FAR):
            z1_out[k, i] = share(k, d).astype(BF16)
        z1[k] = send(z1_out.at[k], z1_in.at[k], z1_s.at[k], z1_r.at[k], to_z(k))
    for i, d in enumerate(NEAR):
        for k in range(ZHI):
            y1_out[i, k] = share(k, d).astype(BF16)
        y1[d] = send(y1_out.at[i], y1_in.at[i], y1_s.at[i], y1_r.at[i], to_y(d))

    gw_ref[...] = jnp.dot(xt[...], g_v[...], preferred_element_type=F32).astype(BF16)
    gb_ref[...] = jnp.sum(g_v[...].astype(F32), axis=0)

    for d in NEAR:
        y1[d].wait_recv()
    for k in Z_OFFSETS:
        s = share(k, 0)
        for i in range(len(NEAR)):
            s = s + y1_in[i, k].astype(F32)
        z2_out[k] = s.astype(BF16)
        z2[k] = send(z2_out.at[k], z2_in.at[k], z2_s.at[k], z2_r.at[k], to_z(k))
    for k in Z_OFFSETS:
        z1[k].wait_recv()
    for i, d in enumerate(FAR):
        s = share(0, d)
        for k in Z_OFFSETS:
            s = s + z1_in[k, i].astype(F32)
        y2_out[i] = s.astype(BF16)
        y2[d] = send(y2_out.at[i], y2_in.at[i], y2_s.at[i], y2_r.at[i], to_y(d))
    s = share(0, 0)
    for i in range(len(NEAR)):
        s = s + y1_in[i, 0].astype(F32)
    for k in (1, 3, 2):
        z2[k].wait_recv()
        s = s + z2_in[k].astype(F32)
    for i, d in reversed(list(enumerate(FAR))):
        y2[d].wait_recv()
        s = s + y2_in[i].astype(F32)
    gi_ref[...] = s.astype(BF16)
    for cp in pending:
        cp.wait_send()


def store(*refs):
    sem = refs[8]
    copies = [pltpu.make_async_copy(refs[i], refs[4 + i], sem.at[i]) for i in range(4)]
    for cp in copies:
        cp.start()
    for cp in copies:
        cp.wait()


def shards(inputs, weight, hidden_bias, cotangent):
    tok, feat = inputs.shape
    hid = weight.shape[1]
    all_tok = tok * COLS
    vmem = pl.BlockSpec(memory_space=pltpu.VMEM)
    hbm = pl.BlockSpec(memory_space=pl.ANY)
    dma = pltpu.SemaphoreType.DMA
    outs = pl.pallas_call(
        kernel,
        out_shape=(
            pltpu.VMEM(cotangent.shape, BF16),
            pltpu.VMEM(inputs.shape, BF16),
            pltpu.VMEM(weight.shape, BF16),
            pltpu.VMEM(hidden_bias.shape, F32),
        ),
        in_specs=[hbm, hbm, vmem, vmem],
        out_specs=(vmem, vmem, vmem, vmem),
        scratch_shapes=[
            pltpu.VMEM((feat, hid), BF16),
            pltpu.VMEM((YS, ZHI, tok, feat), BF16),
            pltpu.VMEM((all_tok, feat), BF16),
            pltpu.VMEM((feat, all_tok), BF16),
            pltpu.VMEM((16, hid), F32),
            pltpu.VMEM((ZHI, 2, 16, hid), F32),
            pltpu.VMEM((ZHI, 2, 16, hid), F32),
            pltpu.VMEM((ZHI, 2, 16, hid), F32),
            pltpu.VMEM((ZHI, 2, 16, hid), BF16),
            pltpu.VMEM((8, 16, hid), BF16),
            pltpu.VMEM((all_tok, hid), BF16),
            pltpu.VMEM((all_tok, feat), F32),
            pltpu.VMEM((4, ZHI, tok, feat), BF16),
            pltpu.VMEM((4, ZHI, tok, feat), BF16),
            pltpu.VMEM((ZHI, 3, tok, feat), BF16),
            pltpu.VMEM((ZHI, 3, tok, feat), BF16),
            pltpu.VMEM((3, tok, feat), BF16),
            pltpu.VMEM((3, tok, feat), BF16),
            pltpu.VMEM((ZHI, tok, feat), BF16),
            pltpu.VMEM((ZHI, tok, feat), BF16),
            dma((2,)),
            dma((ZHI, YS)),
            dma((ZHI, YS)),
            dma((ZHI,)),
            dma((ZHI,)),
            dma((8,)),
            dma((8,)),
            dma((len(CHIPS),)),
            dma((len(CHIPS),)),
            dma((len(CHIPS) + 1,)),
            dma((len(CHIPS) + 1,)),
            dma((4,)),
            dma((4,)),
            dma((ZHI,)),
            dma((ZHI,)),
            dma((3,)),
            dma((3,)),
            dma((ZHI,)),
            dma((ZHI,)),
        ],
        compiler_params=pltpu.CompilerParams(
            collective_id=0, has_side_effects=True, vmem_limit_bytes=32 * 1024 * 1024
        ),
    )(*(pltpu.with_memory_space_constraint(a, pltpu.HBM) for a in (inputs, weight, hidden_bias, cotangent)))
    return pl.pallas_call(
        store,
        out_shape=[pltpu.HBM(o.shape, o.dtype) for o in outs],
        in_specs=[vmem] * 4,
        out_specs=[hbm] * 4,
        scratch_shapes=[dma((4,))],
    )(*(pltpu.with_memory_space_constraint(o, pltpu.VMEM) for o in outs))


def solution(mesh):
    placed = (P("col", "row"), P("row", "col"), P("col"), P("row", "col"))
    return jax.shard_map(
        shards,
        mesh=mesh,
        in_specs=placed,
        out_specs=(P("row", "col"), P("col", "row"), P("row", "col"), P("col")),
        check_vma=False,
    )
```

time: 54.5 us -> 51.3 us (0.941)
  the two profiles are of different devices: /device:TPU:72 before, /device:TPU:1 now
where the time goes in v3:
time: 51.3 us; the launch traced here: 51.1 us
  Pallas kernels  50.5 us (98%)
  between operations  0.64 us (1%)
    pallas_call x1, Pallas kernels, shards(): pl.pallas_call(kernel, out_shape=(pltpu.VMEM(cotangent.shape, BF16), pltp...  49.4 us
    pallas_call x1, Pallas kernels, shards(): pl.pallas_call(store, out_shape=[pltpu.HBM(o.shape, o.dtype) for o in out...  1.07 us

profile of v3, /device:TPU:1, one launch (start us, length us, event | category | flops | bytes accessed | tf_op | source)
XLA Modules:
  0.0 51.1 jit_solution(16936412040638306483)
XLA Ops:
  0.6 49.4 %shard_map.75 = (bf16[16,768]{1,0:T(8,128)(2,1)S(1)}, bf16[8,768]{1,0:T(8,128)(2,1)S(1)}, bf16[768,768]{1,0:T(8,128)(2,1)S(1)}, f32[768]{0:T(1024)S(1)}) custom-call(bf16[8,768]{1,0:T(8,128)(2,1)} %x_hbm.1, bf16[768,768]{1,0:T(8,128)(2,1)} %w_hbm.1, f32[768]{0:T(1024)} %b_ref.1, bf16[16,768]{1,0:T(8,128)(2,1)} %cot_ref.1), custom_call_target="tpu_custom_call" | custom-call | tf_op jit(solution)/shard_map/pallas_call | solution.py:251
  50.0 1.1 %shard_map.76 = (bf16[16,768]{1,0:T(8,128)(2,1)}, bf16[8,768]{1,0:T(8,128)(2,1)}, bf16[768,768]{1,0:T(8,128)(2,1)}, f32[768]{0:T(1024)}) custom-call(bf16[16,768]{1,0:T(8,128)(2,1)S(1)} %get-tuple-element.8.refs_0_, bf16[8,768]{1,0:T(8,128)(2,1)S(1)} %get-tuple-element.9.refs_1_, bf16[768,768]{1,0:T(8,128)(2,1)S(1)} %get-tuple-element.10.refs_2_, ...), custom_call_target="tpu_custom_call" | custom-call | tf_op jit(solution)/shard_map/pallas_call | solution.py:306

commit v4 on v3

--- a/solution.py
+++ b/solution.py
@@ -24,9 +24,9 @@
 
 
 def kernel(
-    x_hbm, w_hbm, b_ref, cot_ref,
+    x_hbm, w_hbm, b_hbm, cot_hbm,
     hid_ref, gi_ref, gw_ref, gb_ref,
-    w_v, xg, xn, xt, mine_f, own, csend, crecv, psend, precv, g_v, part2,
+    w_v, b_v, cot_v, xg, xn, xt, mine_f, own, csend, crecv, psend, precv, g_v, part2,
     y1_out, y1_in, z1_out, z1_in, y2_out, y2_in, z2_out, z2_in,
     local_sem, a_s, a_r, c_s, c_r, p_s, p_r, g_s, g_r, h_s, h_r,
     y1_s, y1_r, z1_s, z1_r, y2_s, y2_r, z2_s, z2_r,
@@ -67,12 +67,15 @@
 
     peers = [to_z(d) for d in Z_OFFSETS] + [to_y(d) for d in FAR + NEAR] + [to_chip(*o) for o in CHIPS] + [other]
     barrier = pltpu.get_barrier_semaphore()
+    x_in = pltpu.make_async_copy(x_hbm, xg.at[y, z], local_sem.at[0])
+    x_in.start()
     for dev in peers:
         pl.semaphore_signal(barrier, inc=1, device_id=dev, device_id_type=MESH)
-    x_in = pltpu.make_async_copy(x_hbm, xg.at[y, z], local_sem.at[0])
     w_in = pltpu.make_async_copy(w_hbm, w_v, local_sem.at[1])
-    x_in.start()
-    w_in.start()
+    b_in = pltpu.make_async_copy(b_hbm, b_v, local_sem.at[2])
+    cot_in = pltpu.make_async_copy(cot_hbm, cot_v, local_sem.at[3])
+    for cp in (w_in, b_in, cot_in):
+        cp.start()
     x_in.wait()
     pl.semaphore_wait(barrier, len(peers))
 
@@ -143,7 +146,8 @@
             def _():
                 mine_f[...] = part
 
-    w_in.wait()
+    for cp in (w_in, b_in, cot_in):
+        cp.wait()
     multiply(0)
     to_owners(0)
     multiply(1)
@@ -154,7 +158,7 @@
     to_owners(2)
 
     xt[...] = xn[...].T
-    v = mine_f[...] + b_ref[...].reshape(1, -1)
+    v = mine_f[...] + b_v[...].reshape(1, -1)
     for d in range(1, 8):
         cp = pltpu.make_async_remote_copy(
             src_ref=psend.at[d // 2, d % 2], dst_ref=precv.at[d], send_sem=p_s.at[d], recv_sem=p_r.at[d],
@@ -166,7 +170,7 @@
 
     mine = pl.ds(pl.multiple_of(r * 16, 16), 16)
     hidden, slope = gelu_and_slope(v)
-    g_v[mine, :] = (cot_ref[...].astype(F32) * slope).astype(BF16)
+    g_v[mine, :] = (cot_v[...].astype(F32) * slope).astype(BF16)
 
     grads, passed = [], []
     for i, (dz, dx) in enumerate(CHIPS):
@@ -202,6 +206,14 @@
     gw_ref[...] = jnp.dot(xt[...], g_v[...], preferred_element_type=F32).astype(BF16)
     gb_ref[...] = jnp.sum(g_v[...].astype(F32), axis=0)
 
+    for k in Z_OFFSETS:
+        z1[k].wait_recv()
+    for i, d in enumerate(FAR):
+        s = share(0, d)
+        for k in Z_OFFSETS:
+            s = s + z1_in[k, i].astype(F32)
+        y2_out[i] = s.astype(BF16)
+        y2[d] = send(y2_out.at[i], y2_in.at[i], y2_s.at[i], y2_r.at[i], to_y(d))
     for d in NEAR:
         y1[d].wait_recv()
     for k in Z_OFFSETS:
@@ -210,14 +222,6 @@
             s = s + y1_in[i, k].astype(F32)
         z2_out[k] = s.astype(BF16)
         z2[k] = send(z2_out.at[k], z2_in.at[k], z2_s.at[k], z2_r.at[k], to_z(k))
-    for k in Z_OFFSETS:
-        z1[k].wait_recv()
-    for i, d in enumerate(FAR):
-        s = share(0, d)
-        for k in Z_OFFSETS:
-            s = s + z1_in[k, i].astype(F32)
-        y2_out[i] = s.astype(BF16)
-        y2[d] = send(y2_out.at[i], y2_in.at[i], y2_s.at[i], y2_r.at[i], to_y(d))
     s = share(0, 0)
     for i in range(len(NEAR)):
         s = s + y1_in[i, 0].astype(F32)
@@ -256,10 +260,12 @@
             pltpu.VMEM(weight.shape, BF16),
             pltpu.VMEM(hidden_bias.shape, F32),
         ),
-        in_specs=[hbm, hbm, vmem, vmem],
+        in_specs=[hbm] * 4,
         out_specs=(vmem, vmem, vmem, vmem),
         scratch_shapes=[
             pltpu.VMEM((feat, hid), BF16),
+            pltpu.VMEM((hid,), F32),
+            pltpu.VMEM((all_tok // ROWS, hid), BF16),
             pltpu.VMEM((YS, ZHI, tok, feat), BF16),
             pltpu.VMEM((all_tok, feat), BF16),
             pltpu.VMEM((feat, all_tok), BF16),
@@ -279,7 +285,7 @@
             pltpu.VMEM((3, tok, feat), BF16),
             pltpu.VMEM((ZHI, tok, feat), BF16),
             pltpu.VMEM((ZHI, tok, feat), BF16),
-            dma((2,)),
+            dma((4,)),
             dma((ZHI, YS)),
             dma((ZHI, YS)),
             dma((ZHI,)),

time: 51.3 us -> 50.4 us (0.982)
  Pallas kernels: 50.5 us -> 49.6 us
    pallas_call x1, Pallas kernels: 49.4 us -> 48.5 us  [shards(): pl.pallas_call(kernel, out_shape=(pltpu.VMEM(cotangent.shape, BF16), pltp...]
where the time goes in v4:
time: 50.4 us; the launch traced here: 50.2 us
  Pallas kernels  49.6 us (98%)
  between operations  0.64 us (1%)
    pallas_call x1, Pallas kernels, shards(): pl.pallas_call(kernel, out_shape=(pltpu.VMEM(cotangent.shape, BF16), pltp...  48.5 us
    pallas_call x1, Pallas kernels, shards(): pl.pallas_call(store, out_shape=[pltpu.HBM(o.shape, o.dtype) for o in out...  1.07 us

profile of v4, /device:TPU:1, one launch (start us, length us, event | category | flops | bytes accessed | tf_op | source)
XLA Modules:
  0.0 50.2 jit_solution(8854694423474738313)
XLA Ops:
  0.6 48.5 %shard_map.75 = (bf16[16,768]{1,0:T(8,128)(2,1)S(1)}, bf16[8,768]{1,0:T(8,128)(2,1)S(1)}, bf16[768,768]{1,0:T(8,128)(2,1)S(1)}, f32[768]{0:T(1024)S(1)}) custom-call(bf16[8,768]{1,0:T(8,128)(2,1)} %x_hbm.1, bf16[768,768]{1,0:T(8,128)(2,1)} %w_hbm.1, f32[768]{0:T(1024)} %b_hbm.1, bf16[16,768]{1,0:T(8,128)(2,1)} %cot_hbm.1), custom_call_target="tpu_custom_call" | custom-call | tf_op jit(solution)/shard_map/pallas_call | solution.py:255
  49.2 1.1 %shard_map.76 = (bf16[16,768]{1,0:T(8,128)(2,1)}, bf16[8,768]{1,0:T(8,128)(2,1)}, bf16[768,768]{1,0:T(8,128)(2,1)}, f32[768]{0:T(1024)}) custom-call(bf16[16,768]{1,0:T(8,128)(2,1)S(1)} %get-tuple-element.8.refs_0_, bf16[8,768]{1,0:T(8,128)(2,1)S(1)} %get-tuple-element.9.refs_1_, bf16[768,768]{1,0:T(8,128)(2,1)S(1)} %get-tuple-element.10.refs_2_, ...), custom_call_target="tpu_custom_call" | custom-call | tf_op jit(solution)/shard_map/pallas_call | solution.py:312

commit v5 on v4

--- a/solution.py
+++ b/solution.py
@@ -152,9 +152,9 @@
     to_owners(0)
     multiply(1)
     multiply(3)
+    multiply(2)
     to_owners(1)
     to_owners(3)
-    multiply(2)
     to_owners(2)
 
     xt[...] = xn[...].T

time: 50.4 us -> 50.5 us (level)
  no operation moved by 1% of the time
where the time goes in v5:
time: 50.5 us; the launch traced here: 50.3 us
  Pallas kernels  49.7 us (98%)
  between operations  0.64 us (1%)
    pallas_call x1, Pallas kernels, shards(): pl.pallas_call(kernel, out_shape=(pltpu.VMEM(cotangent.shape, BF16), pltp...  48.6 us
    pallas_call x1, Pallas kernels, shards(): pl.pallas_call(store, out_shape=[pltpu.HBM(o.shape, o.dtype) for o in out...  1.07 us

profile of v5, /device:TPU:1, one launch (start us, length us, event | category | flops | bytes accessed | tf_op | source)
XLA Modules:
  0.0 50.3 jit_solution(14384168302131998162)
XLA Ops:
  0.6 48.6 %shard_map.75 = (bf16[16,768]{1,0:T(8,128)(2,1)S(1)}, bf16[8,768]{1,0:T(8,128)(2,1)S(1)}, bf16[768,768]{1,0:T(8,128)(2,1)S(1)}, f32[768]{0:T(1024)S(1)}) custom-call(bf16[8,768]{1,0:T(8,128)(2,1)} %x_hbm.1, bf16[768,768]{1,0:T(8,128)(2,1)} %w_hbm.1, f32[768]{0:T(1024)} %b_hbm.1, bf16[16,768]{1,0:T(8,128)(2,1)} %cot_hbm.1), custom_call_target="tpu_custom_call" | custom-call | tf_op jit(solution)/shard_map/pallas_call | solution.py:255
  49.2 1.1 %shard_map.76 = (bf16[16,768]{1,0:T(8,128)(2,1)}, bf16[8,768]{1,0:T(8,128)(2,1)}, bf16[768,768]{1,0:T(8,128)(2,1)}, f32[768]{0:T(1024)}) custom-call(bf16[16,768]{1,0:T(8,128)(2,1)S(1)} %get-tuple-element.8.refs_0_, bf16[8,768]{1,0:T(8,128)(2,1)S(1)} %get-tuple-element.9.refs_1_, bf16[768,768]{1,0:T(8,128)(2,1)S(1)} %get-tuple-element.10.refs_2_, ...), custom_call_target="tpu_custom_call" | custom-call | tf_op jit(solution)/shard_map/pallas_call | solution.py:312
